TPU v7x, 128 devices: a whole 4x4x4 slice. The times are simulated.
128 devices in a mesh: clip: 32 (over y_lo, x, z), stripe: 4 (over y_hi, core).
Axes of the slice: x: 4, y: 4 (y_hi: 2, y_lo: 2; y = y_hi * 2 + y_lo), z: 4, core: 2. Of those that a mesh axis runs over, the one named last changes fastest.
Arguments:
- clip_tokens: bfloat16 [32, 4, 256, 768], P('clip', None, 'stripe'), may hold values from -6 to 6
- timesteps: int32 [32], P('clip'), may hold values from 0 to 999
- loss_weight: float32 [32], P('clip'), may hold values from 0.2 to 5
- cotangent: bfloat16 [32, 4, 256, 768], P('clip', None, 'stripe'), may hold values from -6 to 6
- w_mod: bfloat16 [2, 768, 4608], P(None, None, 'stripe'), may hold values from -0.21875 to 0.21875
- b_mod: bfloat16 [2, 4608], P(None, 'stripe'), may hold values from -3 to 3
- w_qkv: bfloat16 [2, 768, 2304], P(None, 'stripe'), may hold values from -0.21875 to 0.21875
- w_out: bfloat16 [2, 768, 768], P(None, 'stripe'), may hold values from -0.625 to 0.625
- w_up: bfloat16 [2, 768, 3072], P(None, 'stripe'), may hold values from -0.21875 to 0.21875
- b_up: bfloat16 [2, 3072], P(None, 'stripe'), may hold values from -3 to 3
- w_down: bfloat16 [2, 3072, 768], P(None, 'stripe'), may hold values from -0.109375 to 0.109375
Outputs:
- block_output: bfloat16 [32, 4, 256, 768], P('clip', None, 'stripe')
- grad_input: float32 [32, 4, 256, 768], P('clip', None, 'stripe')
- grad_w_mod: float32 [2, 768, 4608], P(None, None, 'stripe')
- grad_b_mod: float32 [2, 4608], P(None, 'stripe')
- grad_w_qkv: float32 [2, 768, 2304], P(None, 'stripe')
- grad_w_out: float32 [2, 768, 768], P(None, 'stripe')
- grad_w_up: float32 [2, 768, 3072], P(None, 'stripe')
- grad_b_up: float32 [2, 3072], P(None, 'stripe')
- grad_w_down: float32 [2, 3072, 768], P(None, 'stripe')
All inputs are finite; a program needn't handle non-finite values.
Results may differ from a plain program's by a relative error of at most 0.033.
Values may be sent and summed in bfloat16 or wider, within the bound.
A program may use at most 192 MiB of HBM per device.

v0:
```python
import math

import jax
import jax.numpy as jnp
from jax import lax
from jax.sharding import PartitionSpec as P

HEAD = 64


spatial_forms = ("fqhe,fkhe->fhqk", "fhqk,fkhe->fqhe", "fhqk,fqhe->fkhe")
temporal_forms = ("qphe,kphe->phqk", "phqk,kphe->qphe", "phqk,qphe->kphe")


def as_sent(x):

    def short(part):
        return part.astype(jnp.bfloat16) if part.dtype == jnp.float32 else part

    return jax.tree.map(short, x)


def norm_rows(values):
    centred = values - jnp.mean(values, axis=-1, keepdims=True)
    spread = jnp.mean(centred * centred, axis=-1, keepdims=True)
    return centred * lax.rsqrt(spread + 1e-06)


def modulate(values, shift, scale):
    return norm_rows(values) * (1.0 + scale) + shift


def gelu_tanh(values):
    return (
        0.5
        * values
        * (1.0 + jnp.tanh(0.7978845608028654 * (values + 0.044715 * values * values * values)))
    )


def silu_plain(values):
    return values / (1.0 + jnp.exp(-values))


def sinusoid(steps, width):
    half = width // 2
    freqs = jnp.exp(-math.log(10000.0) * jnp.arange(half).astype(jnp.float32) / half)
    angles = steps.astype(jnp.float32)[:, None] * freqs[None, :]
    return jnp.concatenate([jnp.cos(angles), jnp.sin(angles)], axis=1)


def trans_dot(left, right):
    return lax.dot_general(
        left, right, (((0,), (0,)), ((), ())), preferred_element_type=jnp.float32
    )


def right_dot(left, right):
    return lax.dot_general(
        left, right, (((1,), (1,)), ((), ())), preferred_element_type=jnp.float32
    )


def fetch_weights(arrays, layer):
    pieces = tuple((a[layer] for a in arrays))
    return jax.tree.map(
        lambda part, own: part.astype(own.dtype),
        lax.all_gather(as_sent(pieces), "stripe", axis=0, tiled=True),
        pieces,
    )


def forward_block(rows, mod, weights, spatial, frames):
    w_qkv, w_out, w_up, b_up, w_down = weights
    shift1, scale1, gate1, shift2, scale2, gate2 = jnp.split(mod, 6)
    width = rows.shape[1]
    heads = width // HEAD
    per_frame = rows.shape[0] // frames
    normed1 = modulate(rows, shift1, scale1).astype(jnp.bfloat16)
    qkv = jnp.dot(normed1, w_qkv, preferred_element_type=jnp.float32).astype(jnp.bfloat16)
    query = qkv[:, :width].reshape(frames, per_frame, heads, HEAD)
    pairs = qkv[:, width:].reshape(frames, per_frame, 2 * width)
    if spatial:
        pairs = lax.all_gather(pairs, "stripe", axis=1, tiled=True)
        forms = spatial_forms
    else:
        forms = temporal_forms
    key = pairs[:, :, :width].reshape(frames, -1, heads, HEAD)
    value = pairs[:, :, width:].reshape(frames, -1, heads, HEAD)
    scale = HEAD ** (-0.5)
    scores = jnp.einsum(forms[0], query, key, preferred_element_type=jnp.float32) * scale
    top = jnp.max(scores, axis=-1, keepdims=True)
    total = jnp.sum(jnp.exp(scores - top), axis=-1, keepdims=True)
    log_total = top + jnp.log(total)
    probs = jnp.exp(scores - log_total).astype(jnp.bfloat16)
    attended = jnp.einsum(forms[1], probs, value, preferred_element_type=jnp.float32)
    attended = attended.reshape(rows.shape[0], width).astype(jnp.bfloat16)
    branch = jnp.dot(attended, w_out, preferred_element_type=jnp.float32)
    mid = rows + gate1 * branch
    normed2 = modulate(mid, shift2, scale2).astype(jnp.bfloat16)
    pre = jnp.dot(normed2, w_up, preferred_element_type=jnp.float32) + b_up.astype(jnp.float32)
    hidden = gelu_tanh(pre).astype(jnp.bfloat16)
    mlp = jnp.dot(hidden, w_down, preferred_element_type=jnp.float32)
    saved = (
        rows,
        normed1,
        query,
        key,
        value,
        log_total,
        attended,
        branch,
        mid,
        normed2,
        pre,
        hidden,
        mlp,
    )
    return (mid + gate2 * mlp, saved)


def backward_block(grad_out, mod, weights, saved, spatial):
    w_qkv, w_out, w_up, b_up, w_down = weights
    (
        rows,
        normed1,
        query,
        key,
        value,
        log_total,
        attended,
        branch,
        mid,
        normed2,
        pre,
        hidden,
        mlp,
    ) = saved
    shift1, scale1, gate1, shift2, scale2, gate2 = jnp.split(mod, 6)
    width = rows.shape[1]
    frames = query.shape[0]
    forms = spatial_forms if spatial else temporal_forms
    grad_gate2 = jnp.sum(grad_out * mlp, axis=0)
    grad_mlp = (gate2 * grad_out).astype(jnp.bfloat16)
    grad_hidden = right_dot(grad_mlp, w_down)
    gelu_pull = jax.vjp(gelu_tanh, pre)[1]
    grad_pre = gelu_pull(grad_hidden)[0].astype(jnp.bfloat16)
    second_pull = jax.vjp(modulate, mid, shift2, scale2)[1]
    grad_mid, grad_shift2, grad_scale2 = second_pull(right_dot(grad_pre, w_up))
    grad_mid = grad_out + grad_mid
    grad_gate1 = jnp.sum(grad_mid * branch, axis=0)
    grad_branch = (gate1 * grad_mid).astype(jnp.bfloat16)
    grad_att = right_dot(grad_branch, w_out).astype(jnp.bfloat16).reshape(query.shape)
    scale = HEAD ** (-0.5)
    scores = jnp.einsum(forms[0], query, key, preferred_element_type=jnp.float32) * scale
    soft = jnp.exp(scores - log_total)
    grad_probs = jnp.einsum(forms[0], grad_att, value, preferred_element_type=jnp.float32)
    centre = jnp.sum(soft * grad_probs, axis=-1, keepdims=True)
    grad_scores = (soft * (grad_probs - centre) * scale).astype(jnp.bfloat16)
    grad_query = jnp.einsum(forms[1], grad_scores, key, preferred_element_type=jnp.float32)
    probs = soft.astype(jnp.bfloat16)
    grad_key = jnp.einsum(forms[2], grad_scores, query, preferred_element_type=jnp.float32)
    grad_value = jnp.einsum(forms[2], probs, grad_att, preferred_element_type=jnp.float32)
    pair_grads = jnp.concatenate(
        [grad_key.reshape(frames, -1, width), grad_value.reshape(frames, -1, width)], axis=2
    )
    if spatial:
        pair_grads = lax.psum_scatter(
            pair_grads.astype(jnp.bfloat16), "stripe", scatter_dimension=1, tiled=True
        ).astype(jnp.float32)
    grad_qkv = jnp.concatenate(
        [grad_query.reshape(-1, width), pair_grads.reshape(-1, 2 * width)], axis=1
    ).astype(jnp.bfloat16)
    first_pull = jax.vjp(modulate, rows, shift1, scale1)[1]
    grad_rows, grad_shift1, grad_scale1 = first_pull(right_dot(grad_qkv, w_qkv))
    grad_rows = grad_mid + grad_rows
    grad_mod = jnp.concatenate(
        [grad_shift1, grad_scale1, grad_gate1, grad_shift2, grad_scale2, grad_gate2]
    )
    activations = (normed1, grad_qkv, attended, grad_branch, normed2, grad_pre, hidden, grad_mlp)
    return (grad_rows, grad_mod, activations)


def group_weight_grads(activations):
    normed1, grad_qkv, attended, grad_branch, normed2, grad_pre, hidden, grad_mlp = activations
    full_sums = (
        trans_dot(normed1, grad_qkv),
        trans_dot(attended, grad_branch),
        trans_dot(normed2, grad_pre),
        jnp.sum(grad_pre.astype(jnp.float32), axis=0),
        trans_dot(hidden, grad_mlp),
    )
    return (
        lax.psum_scatter(
            full_sums[0].astype(jnp.bfloat16), "stripe", scatter_dimension=0, tiled=True
        ).astype(jnp.float32),
        lax.psum_scatter(
            full_sums[1].astype(jnp.bfloat16), "stripe", scatter_dimension=0, tiled=True
        ).astype(jnp.float32),
        lax.psum_scatter(
            full_sums[2].astype(jnp.bfloat16), "stripe", scatter_dimension=0, tiled=True
        ).astype(jnp.float32),
        lax.psum_scatter(
            full_sums[3].astype(jnp.bfloat16), "stripe", scatter_dimension=0, tiled=True
        ).astype(jnp.float32),
        lax.psum_scatter(
            full_sums[4].astype(jnp.bfloat16), "stripe", scatter_dimension=0, tiled=True
        ).astype(jnp.float32),
    )


def shards(
    clip_tokens, timesteps, loss_weight, cotangent, w_mod, b_mod, w_qkv, w_out, w_up, b_up, w_down
):
    frames = clip_tokens.shape[1]
    width = clip_tokens.shape[3]
    count_layers = w_qkv.shape[0]
    arrays = (w_qkv, w_out, w_up, b_up, w_down)
    rows = clip_tokens.reshape(-1, width).astype(jnp.float32)
    embed = silu_plain(sinusoid(timesteps, width)).astype(jnp.bfloat16)
    mod_part = jnp.einsum(
        "d,ldm->lm", embed[0], w_mod, preferred_element_type=jnp.float32
    ) + b_mod.astype(jnp.float32)
    mods = lax.all_gather(mod_part, "stripe", axis=1, tiled=True)
    kept = []
    for layer in range(count_layers):
        weights = fetch_weights(arrays, layer)
        rows, saved = forward_block(rows, mods[layer], weights, layer % 2 == 0, frames)
        kept.append((weights, saved))
    block_output = rows.astype(jnp.bfloat16).reshape(clip_tokens.shape)
    grad = cotangent.reshape(-1, width).astype(jnp.float32) * loss_weight[0]
    grad_mods = [None] * count_layers
    shard_sums = [None] * count_layers
    for layer in reversed(range(count_layers)):
        weights = kept[layer][0]
        grad, grad_mods[layer], activations = backward_block(
            grad, mods[layer], weights, kept[layer][1], layer % 2 == 0
        )
        shard_sums[layer] = group_weight_grads(activations)
    mod_shares = lax.psum_scatter(
        jnp.stack(grad_mods).astype(jnp.bfloat16), "stripe", scatter_dimension=1, tiled=True
    ).astype(jnp.float32)
    stacked = tuple(
        (
            jnp.stack([shard_sums[layer][member] for layer in range(count_layers)])
            for member in range(5)
        )
    )
    grad_w_mod = jnp.einsum("d,lm->ldm", embed[0].astype(jnp.float32), mod_shares)
    totals = (
        lax.psum(grad_w_mod.astype(jnp.bfloat16), "clip").astype(jnp.float32),
        lax.psum(mod_shares.astype(jnp.bfloat16), "clip").astype(jnp.float32),
        lax.psum(stacked[0].astype(jnp.bfloat16), "clip").astype(jnp.float32),
        lax.psum(stacked[1].astype(jnp.bfloat16), "clip").astype(jnp.float32),
        lax.psum(stacked[2].astype(jnp.bfloat16), "clip").astype(jnp.float32),
        lax.psum(stacked[3].astype(jnp.bfloat16), "clip").astype(jnp.float32),
        lax.psum(stacked[4].astype(jnp.bfloat16), "clip").astype(jnp.float32),
    )
    grad_input = grad.reshape(clip_tokens.shape)
    return (
        block_output,
        grad_input,
        totals[0],
        totals[1],
        totals[2],
        totals[3],
        totals[4],
        totals[5],
        totals[6],
    )


def solution(mesh):
    placed = (
        P("clip", None, "stripe", None),
        P("clip"),
        P("clip"),
        P("clip", None, "stripe", None),
        P(None, None, "stripe"),
        P(None, "stripe"),
        P(None, "stripe", None),
        P(None, "stripe", None),
        P(None, "stripe", None),
        P(None, "stripe"),
        P(None, "stripe", None),
    )
    return jax.shard_map(
        shards,
        mesh=mesh,
        in_specs=placed,
        out_specs=(
            P("clip", None, "stripe", None),
            P("clip", None, "stripe", None),
            P(None, None, "stripe"),
            P(None, "stripe"),
            P(None, "stripe", None),
            P(None, "stripe", None),
            P(None, "stripe", None),
            P(None, "stripe"),
            P(None, "stripe", None),
        ),
        check_vma=False,
    )
```

profile of v0, /device:TPU:0, one launch (start us, length us, event | category | flops | bytes accessed | tf_op | source)
XLA Modules:
  0.0 1305.0 jit_solution(15596198773361229987)
XLA Ops:
  16.0 6.7 all_gather.36
  24.3 23.3 %all-gather.22.cloned.1.call-done = bf16[1,768,2304]{2,1,0:T(8,128)(2,1)} async-done(((bf16[1,192,2304]{2,1,0:T(8,128)(2,1)}), bf16[1,768,2304]{2,1,0:T(8,128)(2,1)}) %all-gather.22.cloned.1.call-update) | async-done | bytes 3538960 | tf_op jit(solution)/shard_map/all_gather | solution.py:68
  99.7 7.5 all-gather.24.cloned.1.call-done
  112.2 38.0 %all-gather.26.cloned.1.call-done = bf16[1,768,3072]{2,1,0:T(8,128)(2,1)} async-done(((bf16[1,192,3072]{2,1,0:T(8,128)(2,1)}), bf16[1,768,3072]{2,1,0:T(8,128)(2,1)}) %all-gather.26.cloned.1.call-update) | async-done | bytes 4718608 | tf_op jit(solution)/shard_map/all_gather | solution.py:68
  155.9 37.3 %all-gather.28.cloned.1.call-done = bf16[1,3072,768]{2,1,0:T(8,128)(2,1)} async-done(((bf16[1,768,768]{2,1,0:T(8,128)(2,1)}), bf16[1,3072,768]{2,1,0:T(8,128)(2,1)}) %all-gather.28.cloned.1.call-update) | async-done | bytes 4718608 | tf_op jit(solution)/shard_map/all_gather | solution.py:68
  201.8 27.2 %all-gather.30.cloned.1.call-done = bf16[1,768,2304]{2,1,0:T(8,128)(2,1)} async-done(((bf16[1,192,2304]{2,1,0:T(8,128)(2,1)}), bf16[1,768,2304]{2,1,0:T(8,128)(2,1)}) %all-gather.30.cloned.1.call-update) | async-done | bytes 3538960 | tf_op jit(solution)/shard_map/all_gather | solution.py:68
  260.4 33.9 %all-gather.34.cloned.1.call-done = bf16[1,768,3072]{2,1,0:T(8,128)(2,1)} async-done(((bf16[1,192,3072]{2,1,0:T(8,128)(2,1)}), bf16[1,768,3072]{2,1,0:T(8,128)(2,1)}) %all-gather.34.cloned.1.call-update) | async-done | bytes 4718608 | tf_op jit(solution)/shard_map/all_gather | solution.py:68
  300.0 37.5 %all-gather.36.cloned.1.call-done = bf16[1,3072,768]{2,1,0:T(8,128)(2,1)} async-done(((bf16[1,768,768]{2,1,0:T(8,128)(2,1)}), bf16[1,3072,768]{2,1,0:T(8,128)(2,1)}) %all-gather.36.cloned.1.call-update) | async-done | bytes 4718608 | tf_op jit(solution)/shard_map/all_gather | solution.py:68
  337.4 7.6 fusion.151
  392.9 7.0 fusion.152
  416.6 21.5 %fusion.57 = bf16[4,12,64,256]{3,2,1,0:T(8,128)(2,1)} fusion(bf16[4,64,12,64]{1,3,2,0:T(8,128)(2,1)} %copy.85, f32[4,12,64,256]{3,2,1,0:T(8,128)} %fusion.154, f32[4,12,64,256]{3,2,1,0:T(8,128)S(1)} %get-tuple-element.79, f32[4,12,64]{2,1,0:T(8,128)} %copy-done.51), kind=kOutput, calls=%fused_computation.71 | convolution fusion | flops 108530944 | bytes 8269824 | tf_op jit(solution)/shard_map/fhqk,fqhe->fkhe/dot_general | solution.py:162
  453.3 22.1 %fusion.79 = bf16[4,64,12,64]{1,3,2,0:T(8,128)(2,1)} fusion(bf16[4,256,12,64]{1,3,2,0:T(8,128)(2,1)} %bitcast.189, f32[4,12,64,256]{3,2,1,0:T(8,128)} %fusion.154, f32[4,12,64,256]{3,2,1,0:T(8,128)S(1)} %get-tuple-element.79, f32[4,12,64]{2,1,0:T(8,128)} %copy-done.51), kind=kOutput, calls=%fused_computation.96 | convolution fusion | flops 107941120 | bytes 8269824 | tf_op jit(solution)/shard_map/fhqk,fkhe->fqhe/dot_general | solution.py:160
  479.3 12.2 reduce-scatter.13.cloned.1.call-done
  534.4 26.8 %reduce-scatter.19.cloned.1.call-done = bf16[192,768]{1,0:T(8,128)(2,1)} async-done(((bf16[768,768]{1,0:T(8,128)(2,1)}), bf16[192,768]{1,0:T(8,128)(2,1)}) %reduce-scatter.19.cloned.1.call-update) | async-done | bytes 294928 | tf_op jit(solution)/shard_map/reduce_scatter | solution.py:197
  563.1 33.6 %reduce-scatter.31.cloned.1.call-done = bf16[1152,2]{1,0:T(8,128)(2,1)} async-done(((bf16[4608,2]{1,0:T(8,128)(2,1)}), bf16[1152,2]{1,0:T(8,128)(2,1)}) %reduce-scatter.31.cloned.1.call-update) | async-done | bytes 4624
  600.1 53.3 %reduce-scatter.27.cloned.1.call-done = bf16[768,768]{1,0:T(8,128)(2,1)} async-done(((bf16[3072,768]{1,0:T(8,128)(2,1)}), bf16[768,768]{1,0:T(8,128)(2,1)}) %reduce-scatter.27.cloned.1.call-update) | async-done | bytes 1179664 | tf_op jit(solution)/shard_map/reduce_scatter | solution.py:206
  653.4 57.4 %reduce-scatter.29.cloned.1.call-done = bf16[768,768]{1,0:T(8,128)(2,1)} async-done(((bf16[3072,768]{1,0:T(8,128)(2,1)}), bf16[768,768]{1,0:T(8,128)(2,1)}) %reduce-scatter.29.cloned.1.call-update) | async-done | bytes 1179664 | tf_op jit(solution)/shard_map/reduce_scatter | solution.py:206
  714.1 54.0 %reduce-scatter.23.cloned.1.call-done = bf16[192,3072]{1,0:T(8,128)(2,1)} async-done(((bf16[768,3072]{1,0:T(8,128)(2,1)}), bf16[192,3072]{1,0:T(8,128)(2,1)}) %reduce-scatter.23.cloned.1.call-update) | async-done | bytes 1179664 | tf_op jit(solution)/shard_map/reduce_scatter | solution.py:200
  768.1 57.4 %reduce-scatter.25.cloned.1.call-done = bf16[192,3072]{1,0:T(8,128)(2,1)} async-done(((bf16[768,3072]{1,0:T(8,128)(2,1)}), bf16[192,3072]{1,0:T(8,128)(2,1)}) %reduce-scatter.25.cloned.1.call-update) | async-done | bytes 1179664 | tf_op jit(solution)/shard_map/reduce_scatter | solution.py:200
  828.8 46.1 %reduce-scatter.17.cloned.1.call-done = bf16[192,2304]{1,0:T(8,128)(2,1)} async-done(((bf16[768,2304]{1,0:T(8,128)(2,1)}), bf16[192,2304]{1,0:T(8,128)(2,1)}) %reduce-scatter.17.cloned.1.call-update) | async-done | bytes 884752 | tf_op jit(solution)/shard_map/reduce_scatter | solution.py:194
  874.9 49.6 %reduce-scatter.15.cloned.1.call-done = bf16[192,2304]{1,0:T(8,128)(2,1)} async-done(((bf16[768,2304]{1,0:T(8,128)(2,1)}), bf16[192,2304]{1,0:T(8,128)(2,1)}) %reduce-scatter.15.cloned.1.call-update) | async-done | bytes 884752 | tf_op jit(solution)/shard_map/reduce_scatter | solution.py:194
  929.2 13.4 %all-reduce.4 = (bf16[3072]{0:T(1024)(128)(2,1)S(1)}, bf16[3072]{0:T(1024)(128)(2,1)S(1)}) all-reduce(bf16[3072]{0:T(1024)(128)(2,1)S(1)} %copy-done.102, bf16[3072]{0:T(1024)(128)(2,1)S(1)} %copy-done.103), channel_id=21, replica_groups=mesh['clip'=32,'stripe'=4] {'stripe'}, use_global_device_ids=true, to_apply=%region_50.0.clone | all-reduce | flops 6144 | bytes 24576
  944.0 84.9 %all-reduce.2 = (bf16[2,1152]{1,0:T(2,128)(2,1)S(1)}, bf16[2,768]{1,0:T(2,128)(2,1)S(1)}) all-reduce(bf16[2,1152]{1,0:T(2,128)(2,1)S(1)} %copy.95, bf16[2,768]{1,0:T(2,128)(2,1)S(1)} %pad_maximum_fusion.10), channel_id=1, replica_groups=mesh['clip'=32,'stripe'=4] {'clip'}, use_global_device_ids=true, to_apply=%region_37.0 | all-reduce | flops 3840 | bytes 15360 | tf_op jit(solution)/shard_map/psum | solution.py:252
  1030.1 253.0 %all-reduce.7.cloned.1.call-done = (bf16[2,768,1152]{2,1,0:T(8,128)(2,1)}, bf16[2,192,2304]{2,1,0:T(8,128)(2,1)}, bf16[2,192,768]{2,1,0:T(8,128)(2,1)}, bf16[2,192,3072]{2,1,0:T(8,128)(2,1)}, bf16[2,768,768]{2,1,0:T(8,128)(2,1)}) async-done(((bf16[2,768,1152]{2,1,0:T(8,128)(2,1)}, bf16[2,192,2304]{2,1,0:T(8,128)(2,1)}, bf16[2,192,768]{2,1,0:T(8,128)(2,1)}, bf16[2,192,3072]{2,1,0:T(8,128)(2,1)}, ...) | async-done | bytes 10616848 | tf_op jit(solution)/shard_map/psum | solution.py:251
  (442 shorter events, 275.9 us)
Async XLA Ops:
  7.2 40.4 %all-gather.22.cloned.1.call-start = ((), (), s32[]{:S(2)}) async-start(), calls=%async_computation.20 | async-start | bytes 4423680 | tf_op jit(solution)/shard_map/all_gather | solution.py:68
  10.2 73.8 %all-gather.20.cloned.1.call-start = ((), (), s32[]{:S(2)}) async-start(), calls=%async_computation.10 | async-start | bytes 3932160 | tf_op jit(solution)/shard_map/all_gather | solution.py:84
  24.3 23.4 %copy-start.30 = (bf16[256,768]{1,0:T(8,128)(2,1)}, bf16[256,768]{1,0:T(8,128)(2,1)S(1)}, u32[]{:S(2)}) copy-start(bf16[256,768]{1,0:T(8,128)(2,1)S(1)} %fusion.97) | copy-start | bytes 1179652
  51.7 55.5 %all-gather.24.cloned.1.call-start = ((), (), s32[]{:S(2)}) async-start(), calls=%async_computation.21 | async-start | bytes 1474560 | tf_op jit(solution)/shard_map/all_gather | solution.py:68
  53.6 96.5 %all-gather.26.cloned.1.call-start = ((), (), s32[]{:S(2)}) async-start(), calls=%async_computation.22 | async-start | bytes 5898240 | tf_op jit(solution)/shard_map/all_gather | solution.py:68
  55.3 137.9 %all-gather.28.cloned.1.call-start = ((), (), s32[]{:S(2)}) async-start(), calls=%async_computation.23 | async-start | bytes 5898240 | tf_op jit(solution)/shard_map/all_gather | solution.py:68
  58.5 18.1 %copy-start.49 = (bf16[1,4,64,768]{3,2,1,0:T(8,128)(2,1)S(1)}, bf16[1,4,64,768]{3,2,1,0:T(8,128)(2,1)}, u32[]{:S(2)}) copy-start(bf16[1,4,64,768]{3,2,1,0:T(8,128)(2,1)} %param.14) | copy-start | bytes 1179652
  58.5 18.2 %copy-start.74 = (f32[768]{0:T(1024)S(1)}, f32[768]{0:T(1024)}, u32[]{:S(2)}) copy-start(f32[768]{0:T(1024)} %get-tuple-element.21) | copy-start | bytes 9220
  58.5 170.5 %all-gather.30.cloned.1.call-start = ((), (), s32[]{:S(2)}) async-start(), calls=%async_computation.24 | async-start | bytes 4423680 | tf_op jit(solution)/shard_map/all_gather | solution.py:68
  59.1 196.0 %all-gather.32.cloned.1.call-start = ((), (), s32[]{:S(2)}) async-start(), calls=%async_computation.25 | async-start | bytes 1474560 | tf_op jit(solution)/shard_map/all_gather | solution.py:68
  59.9 234.4 %all-gather.34.cloned.1.call-start = ((), (), s32[]{:S(2)}) async-start(), calls=%async_computation.26 | async-start | bytes 5898240 | tf_op jit(solution)/shard_map/all_gather | solution.py:68
  60.6 276.8 %all-gather.36.cloned.1.call-start = ((), (), s32[]{:S(2)}) async-start(), calls=%async_computation.27 | async-start | bytes 5898240 | tf_op jit(solution)/shard_map/all_gather | solution.py:68
  61.4 430.2 %reduce-scatter.13.cloned.1.call-start = ((), (), s32[]{:S(2)}) async-start(), calls=%async_computation.11 | async-start | bytes 3932160 | tf_op jit(solution)/shard_map/reduce_scatter | solution.py:168
  447.1 87.2 %reduce-scatter.21.cloned.1.call-start = ((), (), s32[]{:S(2)}) async-start(), calls=%async_computation.15 | async-start | bytes 1474560 | tf_op jit(solution)/shard_map/reduce_scatter | solution.py:197
  449.9 111.3 %reduce-scatter.19.cloned.1.call-start = ((), (), s32[]{:S(2)}) async-start(), calls=%async_computation.14 | async-start | bytes 1474560 | tf_op jit(solution)/shard_map/reduce_scatter | solution.py:197
  452.8 143.9 %reduce-scatter.31.cloned.1.call-start = ((), (), s32[]{:S(2)}) async-start(), calls=%async_computation.28 | async-start | bytes 1474560
  499.0 154.4 %reduce-scatter.27.cloned.1.call-start = ((), (), s32[]{:S(2)}) async-start(), calls=%async_computation.18 | async-start | bytes 5898240 | tf_op jit(solution)/shard_map/reduce_scatter | solution.py:206
  505.6 205.2 %reduce-scatter.29.cloned.1.call-start = ((), (), s32[]{:S(2)}) async-start(), calls=%async_computation.19 | async-start | bytes 5898240 | tf_op jit(solution)/shard_map/reduce_scatter | solution.py:206
  512.9 255.2 %reduce-scatter.23.cloned.1.call-start = ((), (), s32[]{:S(2)}) async-start(), calls=%async_computation.16 | async-start | bytes 5898240 | tf_op jit(solution)/shard_map/reduce_scatter | solution.py:200
  519.3 306.3 %reduce-scatter.25.cloned.1.call-start = ((), (), s32[]{:S(2)}) async-start(), calls=%async_computation.17 | async-start | bytes 5898240 | tf_op jit(solution)/shard_map/reduce_scatter | solution.py:200
  525.6 349.3 %reduce-scatter.17.cloned.1.call-start = ((), (), s32[]{:S(2)}) async-start(), calls=%async_computation.13 | async-start | bytes 4423680 | tf_op jit(solution)/shard_map/reduce_scatter | solution.py:194
  530.2 394.3 %reduce-scatter.15.cloned.1.call-start = ((), (), s32[]{:S(2)}) async-start(), calls=%async_computation.12 | async-start | bytes 4423680 | tf_op jit(solution)/shard_map/reduce_scatter | solution.py:194
  534.3 63.6 %copy-start.73 = (f32[768]{0:T(1024)S(1)}, f32[768]{0:T(1024)}, u32[]{:S(2)}) copy-start(f32[768]{0:T(1024)} %get-tuple-element.48) | copy-start | bytes 9220
  534.3 748.8 %all-reduce.7.cloned.1.call-start = ((), (), s32[]{:S(2)}) async-start(), calls=%async_computation.29 | async-start | bytes 21233664 | tf_op jit(solution)/shard_map/psum | solution.py:251
  (116 other events, 498.7 us)
Sparse Core Ops, SparseCore 0:
  10.3 37.2 all-gather.21
  51.8 32.1 all-gather.19
  86.2 20.9 all-gather.23
  109.2 40.9 all-gather.25
  152.3 40.9 all-gather.27
  194.7 34.2 all-gather.29
  230.7 20.9 all-gather.31
  253.3 40.9 all-gather.33
  296.5 40.9 all-gather.35
  447.2 44.3 reduce-scatter.12
  494.5 32.0 reduce-scatter.20
  529.1 32.0 reduce-scatter.18
  564.6 32.0 reduce-scatter.30
  599.2 54.1 reduce-scatter.26
  656.7 54.1 reduce-scatter.28
  713.9 54.1 reduce-scatter.22
  771.4 54.1 reduce-scatter.24
  828.1 46.7 reduce-scatter.16
  877.7 46.7 reduce-scatter.14
  928.4 354.6 all-reduce.6
where the time goes:
time: 1310 us; the launch traced here: 1300 us
  waiting for transfers between devices  855 us (65%)
  matrix products  165 us (13%)
  blocking collectives  118 us (9%)
  local copies, waits for them, and re-layouts  96.2 us (7%)
  other arithmetic  51.4 us (4%)
  between operations  17.7 us (1%)
    psum x1, waiting for transfers between devices, shards(): lax.psum(grad_w_mod.astype(jnp.bfloat16), 'clip').astype(jnp.float32)  253 us
    all_gather x8, waiting for transfers between devices, fetch_weights(): lax.all_gather(as_sent(pieces), 'stripe', axis=0, tiled=True)  205 us
    reduce_scatter x2, waiting for transfers between devices, group_weight_grads(): lax.psum_scatter(full_sums[2].astype(jnp.bfloat16), 'stripe', scatter_dim...  111 us
    reduce_scatter x2, waiting for transfers between devices, group_weight_grads(): lax.psum_scatter(full_sums[4].astype(jnp.bfloat16), 'stripe', scatter_dim...  111 us
    reduce_scatter x2, waiting for transfers between devices, group_weight_grads(): lax.psum_scatter(full_sums[0].astype(jnp.bfloat16), 'stripe', scatter_dim...  95.7 us
    psum x1, blocking collectives, shards(): lax.psum(mod_shares.astype(jnp.bfloat16), 'clip').astype(jnp.float32)  84.9 us
    unnamed x21, waiting for transfers between devices  36.5 us
    dot_general x8, matrix products, trans_dot(): lax.dot_general(left, right, (((0,), (0,)), ((), ())), preferred_element_...  34.4 us
  transfers between devices with their start and end apart: 20, of which 18 were waited for; matrix products, arithmetic and copies ran while one was open for 13% of the time, Pallas kernels for 0%

commit v1 on v0

v1 whole, which is shorter than its diff:
```python
import functools
import math

import jax
import jax.numpy as jnp
from jax import lax
from jax.experimental import pallas as pl
from jax.experimental.pallas import tpu as pltpu
from jax.sharding import PartitionSpec as P

HEAD = 64
MESH = pl.DeviceIdType.MESH
bf16 = jnp.bfloat16
f32 = jnp.float32
spatial_forms = ("fqhe,fkhe->fhqk", "fhqk,fkhe->fqhe", "fhqk,fqhe->fkhe")
temporal_forms = ("qphe,kphe->phqk", "phqk,kphe->qphe", "phqk,qphe->kphe")


class Place:
    def __init__(self):
        clip, stripe = lax.axis_index("clip"), lax.axis_index("stripe")
        self.clip, self.stripe = clip, stripe
        self.ylo = lax.div(clip, 16)
        self.x = lax.rem(lax.div(clip, 4), 4)
        self.z = lax.rem(clip, 4)
        self.yhi = lax.div(stripe, 2)
        self.core = lax.rem(stripe, 2)

    def at_x(self, x):
        return (self.ylo * 16 + x * 4 + self.z, self.stripe)

    def at_z(self, z):
        return (self.ylo * 16 + self.x * 4 + z, self.stripe)

    def ring(self, axis, step):
        there = lax.rem((self.x if axis == 0 else self.z) + step, 4)
        return (self.at_x(there) if axis == 0 else self.at_z(there)), there

    def on_ring(self, axis):
        return self.x if axis == 0 else self.z

    def sibling(self):
        return (self.clip, self.yhi * 2 + 1 - self.core)

    def mirror(self):
        return ((1 - self.ylo) * 16 + self.x * 4 + self.z, (1 - self.yhi) * 2 + self.core)

    def twin(self):
        return ((1 - self.ylo) * 16 + self.x * 4 + self.z, self.stripe)

    def in_group(self, step):
        there = lax.rem(self.stripe + step, 4)
        return (self.clip, there), there


def enter(devices):
    barrier = pltpu.get_barrier_semaphore()
    for device in devices:
        pl.semaphore_signal(barrier, inc=1, device_id=device, device_id_type=MESH)
    pl.semaphore_wait(barrier, len(devices))


class Sems:
    def __init__(self, send, recv):
        self.send, self.recv, self.used = send, recv, 0

    def copy(self, src, dst, device):
        at = self.used
        self.used += 1
        return pltpu.make_async_remote_copy(
            src_ref=src,
            dst_ref=dst,
            send_sem=self.send.at[at],
            recv_sem=self.recv.at[at],
            device_id=device,
            device_id_type=MESH,
        )


def rows_at(start, size, grain):
    return pl.ds(pl.multiple_of(start * grain, grain), size)


def gather_matrix(place, sems, own, full):
    rows, columns = own.shape
    quarter, half = rows // 4, columns // 2
    other = (1 - place.yhi) * 2 + place.core
    parts = []
    for axis in range(2):
        parts.append((axis, pl.ds(axis * half, half)))
    state = {}

    def begin():
        first = []
        for axis, cols in parts:
            mine = rows_at(place.on_ring(axis), quarter, quarter)
            first.append(
                sems.copy(own.at[mine, cols], full.at[place.stripe, mine, cols], place.mirror())
            )
        state["side"] = sems.copy(own, full.at[place.stripe], place.sibling())
        for copy in first:
            copy.start()
        state["side"].start()
        state["first"] = first

    def spread():
        state["ring"] = []
        for axis, cols in parts:
            state["first"][axis].wait()
            mine = rows_at(place.on_ring(axis), quarter, quarter)
            piece = full.at[other, mine, cols]
            for step in (1, 3, 2):
                device, _ = place.ring(axis, step)
                copy = sems.copy(piece, piece, device)
                copy.start()
                state["ring"].append(copy)

    def share():
        state["last"] = []
        for axis, cols in parts:
            for copy in state["ring"][axis * 3 : axis * 3 + 3]:
                copy.wait()
            piece = full.at[other, :, cols]
            copy = sems.copy(piece, piece, place.sibling())
            copy.start()
            state["last"].append(copy)

    def end():
        state["side"].wait()
        for copy in state["last"]:
            copy.wait()

    return begin, spread, share, end


def gather_kernel(
    small, tokens, w_qkv, w_out, w_up, w_down, all_small, frame, q_all, o_all, u_all, d_all,
    send, recv, local
):
    place = Place()
    peers = [place.sibling(), place.mirror()]
    peers += [place.ring(axis, step)[0] for axis in range(2) for step in (1, 2, 3)]
    peers += [(place.clip, lax.rem(place.stripe + 2, 4)), (place.clip, 3 - place.stripe)]
    enter(peers)
    sems = Sems(send, recv)
    quick = []
    for step in (1, 2, 3):
        device, there = place.in_group(step)
        quick.append(sems.copy(small, all_small.at[place.stripe], device))
        quick.append(sems.copy(tokens.at[there], frame.at[place.stripe], device))
    for copy in quick:
        copy.start()
    kept = [
        pltpu.make_async_copy(small, all_small.at[place.stripe], local.at[0]),
        pltpu.make_async_copy(tokens.at[place.stripe], frame.at[place.stripe], local.at[1]),
    ]
    plans = []
    for layer in range(2):
        for member, (own, full) in enumerate(
            ((w_qkv, q_all), (w_out, o_all), (w_up, u_all), (w_down, d_all))
        ):
            plans.append(gather_matrix(place, sems, own.at[layer], full.at[layer]))
            kept.append(
                pltpu.make_async_copy(
                    own.at[layer], full.at[layer, place.stripe], local.at[2 + layer * 4 + member]
                )
            )
    for plan in plans:
        plan[0]()
    for copy in kept:
        copy.start()
    for at in range(len(plans) + 2):
        if at < len(plans):
            plans[at][1]()
        if 0 <= at - 1 < len(plans):
            plans[at - 1][2]()
        if 0 <= at - 2 < len(plans):
            plans[at - 2][3]()
    for copy in quick + kept:
        copy.wait()


def gather(small, tokens, w_qkv, w_out, w_up, w_down):
    anywhere = pl.BlockSpec(memory_space=pl.ANY)
    shapes = [(4, *small.shape), tokens.shape]
    shapes += [(2, 4, *w.shape[1:]) for w in (w_qkv, w_out, w_up, w_down)]
    types = [f32] + [bf16] * 5
    return pl.pallas_call(
        gather_kernel,
        out_shape=[jax.ShapeDtypeStruct(s, t) for s, t in zip(shapes, types)],
        in_specs=[anywhere] * 6,
        out_specs=[anywhere] * 6,
        scratch_shapes=[
            pltpu.SemaphoreType.DMA((94,)),
            pltpu.SemaphoreType.DMA((94,)),
            pltpu.SemaphoreType.DMA((10,)),
        ],
        compiler_params=pltpu.CompilerParams(collective_id=0, has_side_effects=True),
        name="gather_weights",
    )(small, tokens, w_qkv, w_out, w_up, w_down)


def exchange_kernel(source, result, send, recv, local):
    place = Place()
    enter([place.in_group(step)[0] for step in (1, 2, 3)])
    sems = Sems(send, recv)
    copies = []
    for step in (2, 1, 3):
        device, there = place.in_group(step)
        copies.append(sems.copy(source.at[there], result.at[place.stripe], device))
    for copy in copies:
        copy.start()
    kept = pltpu.make_async_copy(source.at[place.stripe], result.at[place.stripe], local)
    kept.start()
    for copy in copies:
        copy.wait()
    kept.wait()


def exchange(blocks, collective_id):
    anywhere = pl.BlockSpec(memory_space=pl.ANY)
    return pl.pallas_call(
        exchange_kernel,
        out_shape=jax.ShapeDtypeStruct(blocks.shape, blocks.dtype),
        in_specs=[anywhere],
        out_specs=anywhere,
        scratch_shapes=[
            pltpu.SemaphoreType.DMA((3,)),
            pltpu.SemaphoreType.DMA((3,)),
            pltpu.SemaphoreType.DMA,
        ],
        compiler_params=pltpu.CompilerParams(collective_id=collective_id, has_side_effects=True),
        name="exchange_rows",
    )(blocks)


CHUNKS = 6
STAGES = 8


def add_into(out, *terms, rows=64):
    height = out.shape[0]
    rows = min(rows, height)

    @pl.loop(0, height // rows)
    def _(step):
        at = pl.ds(pl.multiple_of(step * rows, rows), rows)
        total = terms[0][at, :].astype(f32)
        for term in terms[1:]:
            total = total + term[at, :].astype(f32)
        out[at, :] = total.astype(out.dtype)


class Reduce:
    def __init__(self, place, bufs, outs):
        self.place, self.bufs, self.outs = place, bufs, outs
        self.flight = {}

    def sems(self, k, base):
        send, recv = self.bufs["send"], self.bufs["recv"]
        sems = Sems(send.at[k % 2], recv.at[k % 2])
        sems.used = base
        return sems

    def go(self, key, copies):
        for copy in copies:
            copy.start()
        self.flight[key] = copies

    def land(self, key):
        for copy in self.flight.pop(key):
            copy.wait()

    def cols(self, axis):
        return pl.ds(axis * 384, 384)

    def step(self, stage, k):
        place, b, bufs = self.place, k % 2, self.bufs
        sib_core = 1 - place.core
        if stage == 0:
            sems = self.sems(k, 0)
            grads = bufs["grads"].at[k]
            own = [
                pltpu.make_async_copy(
                    grads.at[2 * h + place.core], bufs["part"].at[b, h], bufs["local"].at[b, h]
                )
                for h in range(2)
            ]
            for copy in own:
                copy.start()
            self.flight["own", k] = own
            self.go(
                (0, k),
                [
                    sems.copy(grads.at[2 * h + sib_core], bufs["side"].at[b, h], place.sibling())
                    for h in range(2)
                ],
            )
        elif stage == 1:
            self.land((0, k))
            self.land(("own", k))
            for h in range(2):
                part = bufs["part"].at[b, h]
                add_into(part, part, bufs["side"].at[b, h])
            sems = self.sems(k, 2)
            copies = []
            for step in (1, 3, 2):
                for axis in range(2):
                    device, there = place.ring(axis, step)
                    piece = bufs["part"].at[b, :, rows_at(there, 192, 192), self.cols(axis)]
                    copies.append(sems.copy(piece, bufs["ring"].at[b, axis, step - 1], device))
            self.go((1, k), copies)
        elif stage == 2:
            self.land((1, k))
            for axis in range(2):
                mine = rows_at(place.on_ring(axis), 192, 192)
                for h in range(2):
                    add_into(
                        bufs["sums"].at[b, h, axis],
                        bufs["part"].at[b, h, mine, self.cols(axis)],
                        *[bufs["ring"].at[b, axis, step, h] for step in range(3)],
                    )
            sems = self.sems(k, 8)
            self.go(
                (2, k),
                [sems.copy(bufs["sums"].at[b, 1 - place.yhi], bufs["cross"].at[b], place.mirror())],
            )
        elif stage == 3:
            self.land((2, k))
            sems = self.sems(k, 9)
            copies = []
            for axis in range(2):
                ours = bufs["ours"].at[b, axis]
                add_into(ours, bufs["sums"].at[b, place.yhi, axis], bufs["cross"].at[b, axis])
            for step in (1, 3, 2):
                for axis in range(2):
                    device, there = place.ring(1 - axis, step)
                    piece = bufs["ours"].at[b, axis, rows_at(there, 48, 48)]
                    copies.append(sems.copy(piece, bufs["ring2"].at[b, axis, step - 1], device))
            self.go((3, k), copies)
        elif stage == 4:
            self.land((3, k))
            for axis in range(2):
                mine = rows_at(place.on_ring(1 - axis), 48, 48)
                add_into(
                    bufs["small"].at[b, axis],
                    bufs["ours"].at[b, axis, mine],
                    *[bufs["ring2"].at[b, axis, step] for step in range(3)],
                    rows=48,
                )
            sems = self.sems(k, 15)
            self.go((4, k), [sems.copy(bufs["small"].at[b], bufs["twin"].at[b], place.twin())])
        elif stage == 5:
            self.land((4, k))
            sems = self.sems(k, 16)
            copies = []
            pieces = []
            for axis in range(2):
                start = place.on_ring(axis) * 192 + place.on_ring(1 - axis) * 48
                piece = bufs["final"].at[k, rows_at(start // 16, 48, 16), self.cols(axis)]
                add_into(piece, bufs["small"].at[b, axis], bufs["twin"].at[b, axis], rows=48)
                pieces.append(piece)
            for step in (1, 3, 2):
                for axis in range(2):
                    device, _ = place.ring(1 - axis, step)
                    copies.append(sems.copy(pieces[axis], pieces[axis], device))
            self.go((5, k), copies)
        elif stage == 6:
            self.land((5, k))
            sems = self.sems(k, 22)
            copies = []
            for step in (1, 3, 2):
                for axis in range(2):
                    device, _ = place.ring(axis, step)
                    mine = rows_at(place.on_ring(axis), 192, 192)
                    piece = bufs["final"].at[k, mine, self.cols(axis)]
                    copies.append(sems.copy(piece, piece, device))
            self.go((6, k), copies)
        else:
            self.land((6, k))
            copies = []
            layer, member = 1 - k // 3, k % 3
            out_qkv, out_out, out_up, out_down = self.outs
            for j in range(4):
                block = bufs["final"].at[k, pl.ds(j * 192, 192)]
                wide = pl.ds(j * 768, 768)
                if member == 0:
                    to = out_down.at[layer, pl.ds(j * 192, 192)]
                elif member == 1:
                    to = out_up.at[layer, :, wide]
                elif j < 3:
                    to = out_qkv.at[layer, :, wide]
                else:
                    to = out_out.at[layer]
                copies.append(pltpu.make_async_copy(block, to, bufs["store"].at[k, j]))
            self.go(("store", k), copies)


class ReduceSmall:
    def __init__(self, place, bufs, send, recv, out):
        self.place, self.bufs, self.out = place, bufs, out
        self.sems = Sems(send, recv)

    def go(self, copies):
        for copy in copies:
            copy.start()
        self.flight = copies

    def land(self):
        for copy in self.flight:
            copy.wait()

    def step(self, stage):
        place, bufs, sems = self.place, self.bufs, self.sems
        if stage == 0:
            copies = []
            for step in (1, 2, 3):
                device, there = place.in_group(step)
                copies.append(sems.copy(bufs["in"].at[there], bufs["land"].at[step - 1], device))
            self.go(copies)
        elif stage == 1:
            self.land()
            total = bufs["in"][place.stripe]
            for step in range(3):
                total = total + bufs["land"][step]
            mine = bufs["all"].at[place.ylo, place.x, place.z]
            mine[...] = total.astype(bf16)
            self.go([sems.copy(mine, mine, place.ring(0, step)[0]) for step in (1, 2, 3)])
        elif stage == 2:
            self.land()
            mine = bufs["all"].at[place.ylo, :, place.z]
            self.go([sems.copy(mine, mine, place.ring(1, step)[0]) for step in (1, 2, 3)])
        elif stage == 3:
            self.land()
            mine = bufs["all"].at[place.ylo]
            self.go([sems.copy(mine, mine, place.twin())])
        elif stage == 4:
            self.land()


REDUCE_SCRATCH = {
    "part": ((2, 2, 768, 768), bf16),
    "side": ((2, 2, 768, 768), bf16),
    "ring": ((2, 2, 3, 2, 192, 384), bf16),
    "sums": ((2, 2, 2, 192, 384), bf16),
    "cross": ((2, 2, 192, 384), bf16),
    "ours": ((2, 2, 192, 384), bf16),
    "ring2": ((2, 2, 3, 48, 384), bf16),
    "small": ((2, 2, 48, 384), bf16),
    "twin": ((2, 2, 48, 384), bf16),
    "final": ((CHUNKS, 768, 768), bf16),
}
REDUCE_SEMS = {"send": (2, 28), "recv": (2, 28), "local": (2, 2), "store": (CHUNKS, 4)}


def reduce_peers(place):
    peers = [place.sibling(), place.mirror(), place.twin()]
    peers += [place.ring(axis, step)[0] for axis in range(2) for step in (1, 2, 3)]
    peers += [(place.clip, lax.rem(place.stripe + 2, 4)), (place.clip, 3 - place.stripe)]
    return peers


def reduce_kernel(grads, small_in, out_qkv, out_out, out_up, out_down, small_out, *scratch):
    place = Place()
    names = list(REDUCE_SCRATCH) + list(REDUCE_SEMS)
    bufs = dict(zip(names, scratch))
    land, everything, small_send, small_recv = scratch[len(names) :]
    bufs["grads"] = grads
    enter(reduce_peers(place))
    reduce = Reduce(place, bufs, (out_qkv, out_out, out_up, out_down))
    small = ReduceSmall(
        place, {"in": small_in, "land": land, "all": small_out}, small_send, small_recv, small_out
    )
    for slot in range(CHUNKS + STAGES - 1):
        for stage in reversed(range(STAGES)):
            if 0 <= slot - stage < CHUNKS:
                reduce.step(stage, slot - stage)
        if slot < 5:
            small.step(slot)
    for k in range(CHUNKS):
        reduce.land(("store", k))


def reduce_all(grads, small):
    anywhere = pl.BlockSpec(memory_space=pl.ANY)
    vmem = pl.BlockSpec(memory_space=pltpu.VMEM)
    scratch = [pltpu.VMEM(*spec) for spec in REDUCE_SCRATCH.values()]
    scratch += [pltpu.SemaphoreType.DMA(shape) for shape in REDUCE_SEMS.values()]
    scratch += [
        pltpu.VMEM((3, 16, 384), f32),
        pltpu.VMEM((8, 128), f32),
        pltpu.SemaphoreType.DMA((10,)),
        pltpu.SemaphoreType.DMA((10,)),
    ]
    shapes = [(2, 192, 2304), (2, 192, 768), (2, 192, 3072), (2, 768, 768), (2, 4, 4, 16, 384)]
    return pl.pallas_call(
        reduce_kernel,
        out_shape=[jax.ShapeDtypeStruct(s, bf16) for s in shapes],
        in_specs=[anywhere, vmem],
        out_specs=[anywhere] * 4 + [vmem],
        scratch_shapes=scratch,
        compiler_params=pltpu.CompilerParams(
            collective_id=4, has_side_effects=True, vmem_limit_bytes=56 * 2**20
        ),
        name="reduce_gradients",
    )(grads, small)


def norm_rows(values):
    centred = values - jnp.mean(values, axis=-1, keepdims=True)
    spread = jnp.mean(centred * centred, axis=-1, keepdims=True)
    return centred * lax.rsqrt(spread + 1e-06)


def modulate(values, shift, scale):
    return norm_rows(values) * (1.0 + scale) + shift


def gelu_tanh(values):
    return (
        0.5
        * values
        * (1.0 + jnp.tanh(0.7978845608028654 * (values + 0.044715 * values * values * values)))
    )


def silu_plain(values):
    return values / (1.0 + jnp.exp(-values))


def sinusoid(steps, width):
    half = width // 2
    freqs = jnp.exp(-math.log(10000.0) * jnp.arange(half).astype(f32) / half)
    angles = steps.astype(f32)[:, None] * freqs[None, :]
    return jnp.concatenate([jnp.cos(angles), jnp.sin(angles)], axis=1)


def trans_dot(left, right):
    return lax.dot_general(left, right, (((0,), (0,)), ((), ())), preferred_element_type=f32)


def right_dot(left, right):
    return lax.dot_general(left, right, (((1,), (1,)), ((), ())), preferred_element_type=f32)


def forward_block(rows, mod, weights, spatial):
    w_qkv, w_out, w_up, b_up, w_down = weights
    shift1, scale1, gate1, shift2, scale2, gate2 = jnp.split(mod, 6)
    width = rows.shape[1]
    heads = width // HEAD
    frames = 1 if spatial else 4
    per_frame = rows.shape[0] // frames
    normed1 = modulate(rows, shift1, scale1).astype(bf16)
    qkv = jnp.dot(normed1, w_qkv, preferred_element_type=f32).astype(bf16)
    forms = spatial_forms if spatial else temporal_forms
    query, key, value = (
        qkv[:, i * width : (i + 1) * width].reshape(frames, per_frame, heads, HEAD)
        for i in range(3)
    )
    scale = HEAD ** (-0.5)
    scores = jnp.einsum(forms[0], query, key, preferred_element_type=f32) * scale
    top = jnp.max(scores, axis=-1, keepdims=True)
    total = jnp.sum(jnp.exp(scores - top), axis=-1, keepdims=True)
    log_total = top + jnp.log(total)
    probs = jnp.exp(scores - log_total).astype(bf16)
    attended = jnp.einsum(forms[1], probs, value, preferred_element_type=f32)
    attended = attended.reshape(rows.shape[0], width).astype(bf16)
    branch = jnp.dot(attended, w_out, preferred_element_type=f32)
    mid = rows + gate1 * branch
    normed2 = modulate(mid, shift2, scale2).astype(bf16)
    pre = jnp.dot(normed2, w_up, preferred_element_type=f32) + b_up
    hidden = gelu_tanh(pre).astype(bf16)
    mlp = jnp.dot(hidden, w_down, preferred_element_type=f32)
    saved = (
        rows, normed1, query, key, value, log_total, attended, branch, mid, normed2, pre, hidden,
        mlp
    )
    return (mid + gate2 * mlp, saved)


def backward_block(grad_out, mod, weights, saved, spatial):
    w_qkv, w_out, w_up, b_up, w_down = weights
    (
        rows, normed1, query, key, value, log_total, attended, branch, mid, normed2, pre, hidden,
        mlp
    ) = saved
    shift1, scale1, gate1, shift2, scale2, gate2 = jnp.split(mod, 6)
    width = rows.shape[1]
    forms = spatial_forms if spatial else temporal_forms
    grad_gate2 = jnp.sum(grad_out * mlp, axis=0)
    grad_mlp = (gate2 * grad_out).astype(bf16)
    grad_hidden = right_dot(grad_mlp, w_down)
    gelu_pull = jax.vjp(gelu_tanh, pre)[1]
    grad_pre = gelu_pull(grad_hidden)[0].astype(bf16)
    second_pull = jax.vjp(modulate, mid, shift2, scale2)[1]
    grad_mid, grad_shift2, grad_scale2 = second_pull(right_dot(grad_pre, w_up))
    grad_mid = grad_out + grad_mid
    grad_gate1 = jnp.sum(grad_mid * branch, axis=0)
    grad_branch = (gate1 * grad_mid).astype(bf16)
    grad_att = right_dot(grad_branch, w_out).astype(bf16).reshape(query.shape)
    scale = HEAD ** (-0.5)
    scores = jnp.einsum(forms[0], query, key, preferred_element_type=f32) * scale
    soft = jnp.exp(scores - log_total)
    grad_probs = jnp.einsum(forms[0], grad_att, value, preferred_element_type=f32)
    centre = jnp.sum(soft * grad_probs, axis=-1, keepdims=True)
    grad_scores = (soft * (grad_probs - centre) * scale).astype(bf16)
    grad_query = jnp.einsum(forms[1], grad_scores, key, preferred_element_type=f32)
    probs = soft.astype(bf16)
    grad_key = jnp.einsum(forms[2], grad_scores, query, preferred_element_type=f32)
    grad_value = jnp.einsum(forms[2], probs, grad_att, preferred_element_type=f32)
    grad_qkv = jnp.concatenate(
        [g.reshape(-1, width) for g in (grad_query, grad_key, grad_value)], axis=1
    ).astype(bf16)
    first_pull = jax.vjp(modulate, rows, shift1, scale1)[1]
    grad_rows, grad_shift1, grad_scale1 = first_pull(right_dot(grad_qkv, w_qkv))
    grad_rows = grad_mid + grad_rows
    grad_mod = jnp.concatenate(
        [grad_shift1, grad_scale1, grad_gate1, grad_shift2, grad_scale2, grad_gate2]
    )

    def wide(grad):
        blocks = grad.shape[1] // 768
        return grad.astype(bf16).reshape(4, 192, blocks, 768).transpose(0, 2, 1, 3).reshape(
            4, 192 * blocks, 768
        )

    chunks = [
        trans_dot(hidden, grad_mlp).astype(bf16).reshape(4, 768, 768),
        wide(trans_dot(normed2, grad_pre)),
        jnp.concatenate(
            [
                wide(trans_dot(normed1, grad_qkv)),
                wide(trans_dot(attended, grad_branch)),
            ],
            axis=1,
        ),
    ]
    grad_b_up = jnp.sum(grad_pre.astype(f32), axis=0)
    return (grad_rows, grad_mod, grad_b_up, chunks)


def shards(
    clip_tokens, timesteps, loss_weight, cotangent, w_mod, b_mod, w_qkv, w_out, w_up, b_up, w_down
):
    width = clip_tokens.shape[3]
    embed = silu_plain(sinusoid(timesteps, width)).astype(bf16)
    mod_part = jnp.einsum("d,ldm->lm", embed[0], w_mod, preferred_element_type=f32) + b_mod.astype(
        f32
    )
    small = jnp.concatenate([b_up.astype(f32).reshape(4, 384), mod_part.reshape(6, 384)])
    small = jnp.pad(small, ((0, 6), (0, 0)))
    all_small, frame, *full = gather(small, clip_tokens[0], w_qkv, w_out, w_up, w_down)
    b_ups = all_small[:, 0:4].reshape(4, 2, 768).transpose(1, 0, 2).reshape(2, 3072)
    mods = all_small[:, 4:10].reshape(4, 2, 1152).transpose(1, 0, 2).reshape(2, 4608)
    weights = [
        (
            full[0][layer].reshape(768, 2304),
            full[1][layer].reshape(768, 768),
            full[2][layer].reshape(768, 3072),
            b_ups[layer],
            full[3][layer].reshape(3072, 768),
        )
        for layer in range(2)
    ]
    rows, saved0 = forward_block(frame.reshape(256, width).astype(f32), mods[0], weights[0], True)
    rows = exchange(rows.astype(bf16).reshape(4, 64, width), 1).reshape(256, width).astype(f32)
    rows, saved1 = forward_block(rows, mods[1], weights[1], False)
    block_output = rows.astype(bf16).reshape(clip_tokens.shape)
    grad = cotangent.reshape(-1, width).astype(f32) * loss_weight[0]
    grad, mod1, b_up1, chunks1 = backward_block(grad, mods[1], weights[1], saved1, False)
    grad = exchange(grad.astype(bf16).reshape(4, 64, width), 2).reshape(256, width).astype(f32)
    grad, mod0, b_up0, chunks0 = backward_block(grad, mods[0], weights[0], saved0, True)
    grad = exchange(grad.astype(bf16).reshape(4, 64, width), 3)
    grad_input = grad.astype(f32).reshape(clip_tokens.shape)

    b_part = jnp.stack([b_up0, b_up1]).reshape(2, 4, 768).transpose(1, 0, 2).reshape(4, 4, 384)
    m_part = jnp.stack([mod0, mod1]).reshape(2, 4, 1152).transpose(1, 0, 2).reshape(4, 6, 384)
    e_part = jnp.broadcast_to(0.25 * embed.astype(f32).reshape(1, 2, 384), (4, 2, 384))
    small = jnp.concatenate([b_part, m_part, e_part, jnp.zeros((4, 4, 384), f32)], axis=1)
    *sums, everyone = reduce_all(jnp.stack(chunks1 + chunks0), small)
    everyone = everyone.reshape(32, 16, 384)
    b_all = everyone[:, 0:4].astype(f32).sum(0).reshape(2, 768)
    m_all = everyone[:, 4:10].reshape(32, 2, 1152)
    e_all = everyone[:, 10:12].reshape(32, 768)
    grad_w_mod = jnp.einsum("cd,clm->ldm", e_all, m_all, preferred_element_type=f32)
    return (
        block_output,
        grad_input,
        grad_w_mod,
        m_all.astype(f32).sum(0),
        sums[0].astype(f32),
        sums[1].astype(f32),
        sums[2].astype(f32),
        b_all,
        sums[3].astype(f32),
    )


def solution(mesh):
    placed = (
        P("clip", None, "stripe", None),
        P("clip"),
        P("clip"),
        P("clip", None, "stripe", None),
        P(None, None, "stripe"),
        P(None, "stripe"),
        P(None, "stripe", None),
        P(None, "stripe", None),
        P(None, "stripe", None),
        P(None, "stripe"),
        P(None, "stripe", None),
    )
    return jax.shard_map(
        shards,
        mesh=mesh,
        in_specs=placed,
        out_specs=(
            P("clip", None, "stripe", None),
            P("clip", None, "stripe", None),
            P(None, None, "stripe"),
            P(None, "stripe"),
            P(None, "stripe", None),
            P(None, "stripe", None),
            P(None, "stripe", None),
            P(None, "stripe"),
            P(None, "stripe", None),
        ),
        check_vma=False,
    )
```

time: 1310 us -> 748 us (0.57)
  waiting for transfers between devices: 855 us -> 0 us
  Pallas kernels: 0 us -> 412 us
  blocking collectives: 118 us -> 0 us
  local copies, waits for them, and re-layouts: 96.2 us -> 147 us
  matrix products: 165 us -> 128 us
  between operations: 17.7 us -> 4.04 us
    pallas_call x0 -> x5, Pallas kernels: none -> 412 us  [the longest x1 225 us: gather(): pl.pallas_call(gather_kernel, out_shape=[jax.ShapeDtypeStruct(s, t) for s...]
    reduce_scatter x9 -> x0, waiting for transfers between devices: 357 us -> none  [the longest x2 111 us: group_weight_grads(): lax.psum_scatter(full_sums[2].astype(jnp.bfloat16), 'stripe', scatter_dim...]
    psum x1 -> x0, waiting for transfers between devices: 253 us -> none  [shards(): lax.psum(grad_w_mod.astype(jnp.bfloat16), 'clip').astype(jnp.float32)]
    all_gather x9 -> x0, waiting for transfers between devices: 209 us -> none  [the longest x8 205 us: fetch_weights(): lax.all_gather(as_sent(pieces), 'stripe', axis=0, tiled=True)]
    psum x1 -> x0, blocking collectives: 84.9 us -> none  [shards(): lax.psum(mod_shares.astype(jnp.bfloat16), 'clip').astype(jnp.float32)]
    dot_general x21 -> x22, matrix products: 101 us -> 63.5 us  [the longest x2 8.55 us: backward_block(): jnp.einsum(forms[2], grad_scores, query, preferred_element_type=f32)]
    unnamed x21 -> x0, waiting for transfers between devices: 36.5 us -> none
    reshape x13 -> x22, local copies, waits for them, and re-layouts: 28.1 us -> 54 us  [the longest x6 36.7 us: wide(): grad.astype(bf16).reshape(4, 192, blocks, 768).transpose(0, 2, 1, 3)]
  transfers between devices with their start and end apart: 20 -> 0, of which waited for: 18 -> 0; matrix products, arithmetic and copies ran while one was open for 13% -> 0% of each run, Pallas kernels for 0% -> 0%
where the time goes in v1:
time: 748 us; the launch traced here: 743 us
  Pallas kernels  412 us (55%)
  local copies, waits for them, and re-layouts  147 us (20%)
  matrix products  128 us (17%)
  other arithmetic  51.6 us (7%)
    pallas_call x1, Pallas kernels, gather(): pl.pallas_call(gather_kernel, out_shape=[jax.ShapeDtypeStruct(s, t) for s...  225 us
    pallas_call x1, Pallas kernels, reduce_all(): pl.pallas_call(reduce_kernel, out_shape=[jax.ShapeDtypeStruct(s, bf16) fo...  161 us
    dot_general x8, matrix products, right_dot(): lax.dot_general(left, right, (((1,), (1,)), ((), ())), preferred_element_...  45.6 us
    reshape x6, local copies, waits for them, and re-layouts, wide(): grad.astype(bf16).reshape(4, 192, blocks, 768).transpose(0, 2, 1, 3)  36.7 us
    unnamed x211, local copies, waits for them, and re-layouts  30.5 us
    pallas_call x3, Pallas kernels, exchange(): pl.pallas_call(exchange_kernel, out_shape=jax.ShapeDtypeStruct(blocks.sha...  26 us
    dot_general x8, matrix products, trans_dot(): lax.dot_general(left, right, (((0,), (0,)), ((), ())), preferred_element_...  19.4 us

profile of v1, /device:TPU:0, one launch (start us, length us, event | category | flops | bytes accessed | tf_op | source)
XLA Modules:
  0.0 742.6 jit_solution(984394851779092769)
XLA Ops:
  3.9 225.2 %gather_weights.1 = (f32[4,16,384]{2,1,0:T(8,128)}, bf16[4,64,768]{2,1,0:T(8,128)(2,1)}, bf16[2,4,192,2304]{3,2,1,0:T(8,128)(2,1)}, bf16[2,4,192,768]{3,2,1,0:T(...) custom-call(f32[16,384]{1,0:T(8,128)} %select_maximum_fusion.small, ...), custom_call_target="tpu_custom_call" | custom-call | tf_op jit(solution)/shard_map/gather_weights/pallas_call | solution.py:188
  236.8 5.3 fusion.124
  256.3 8.1 %fusion.123 = (bf16[1,4,768,768]{3,2,1,0:T(8,128)(2,1)}, bf16[1,4,768,768]{3,2,1,0:T(8,128)(2,1)}) fusion(bf16[2,4,768,768]{3,2,1,0:T(8,128)(2,1)} %get-tuple-element.25), kind=kLoop, calls=%fused_computation.245 | loop fusion | bytes 18874368 | tf_op jit(solution)/shard_map/slice | solution.py:661
  264.5 8.4 %fusion.122 = (bf16[1,4,192,3072]{3,2,1,0:T(8,128)(2,1)}, bf16[1,4,192,3072]{3,2,1,0:T(8,128)(2,1)}) fusion(bf16[2,4,192,3072]{3,2,1,0:T(8,128)(2,1)} %get-tuple-element.24), kind=kLoop, calls=%fused_computation.244 | loop fusion | bytes 18874368 | tf_op jit(solution)/shard_map/slice | solution.py:659
  276.5 4.1 convolution_add_fusion.1
  284.0 8.7 %exchange_rows.3 = bf16[4,64,768]{2,1,0:T(8,128)(2,1)} custom-call(bf16[4,64,768]{2,1,0:T(8,128)(2,1)} %bitcast.272), custom_call_target="tpu_custom_call" | custom-call | tf_op jit(solution)/shard_map/exchange_rows/pallas_call | solution.py:222
  322.8 4.0 convolution_add_fusion
  326.8 15.6 %convert_reduce_fusion = (f32[3072]{0:T(1024)}, bf16[256,3072]{1,0:T(8,128)(2,1)S(1)}) fusion(f32[256,3072]{1,0:T(8,128)S(1)} %convolution_add_fusion, bf16[256,768]{1,0:T(8,128)(2,1)S(1)} %bitcast.274, bf16[3072,768]{1,0:T(8,128)(2,1)S(1)} %bitcast.243), kind=kOutput, calls=%fused_computation.37 | convolution fusion | flops 1228403712 | bytes 9842688 | tf_op jit(solution)/shard_map/dot_general | solution.py:543
  391.3 4.9 fusion.61
  403.6 8.6 %exchange_rows.4 = bf16[4,64,768]{2,1,0:T(8,128)(2,1)} custom-call(bf16[4,64,768]{2,1,0:T(8,128)(2,1)} %bitcast.259), custom_call_target="tpu_custom_call" | custom-call | tf_op jit(solution)/shard_map/exchange_rows/pallas_call | solution.py:222
  413.3 8.6 %convert_reduce_fusion.1 = (f32[3072]{0:T(1024)}, bf16[256,3072]{1,0:T(8,128)(2,1)S(1)}) fusion(f32[256,3072]{1,0:T(8,128)} %copy-done.87, bf16[256,768]{1,0:T(8,128)(2,1)S(1)} %bitcast.271, bf16[3072,768]{1,0:T(8,128)(2,1)} %bitcast.237), kind=kOutput, calls=%fused_computation.38 | convolution fusion | flops 1228403712 | bytes 9842688 | tf_op jit(solution)/shard_map/dot_general | solution.py:543
  422.0 5.2 multiply_reduce_fusion.5
  440.3 5.3 fusion.38
  445.6 5.2 fusion.35
  457.5 8.6 %exchange_rows.5 = bf16[4,64,768]{2,1,0:T(8,128)(2,1)} custom-call(bf16[4,64,768]{2,1,0:T(8,128)(2,1)} %bitcast.260), custom_call_target="tpu_custom_call" | custom-call | tf_op jit(solution)/shard_map/exchange_rows/pallas_call | solution.py:222
  468.1 4.1 convolution_convert_fusion.5
  478.7 9.7 %reshape.595 = bf16[4,192,4,768]{3,2,1,0:T(4,128)(2,1)} reshape(bf16[768,3072]{1,0:T(8,128)(2,1)} %convolution_convert_fusion.4) | data formatting | bytes 9437184 | tf_op jit(solution)/shard_map/reshape | solution.py:623
  496.8 5.3 reshape.596
  517.4 9.9 %reshape.598 = bf16[4,192,4,768]{3,2,1,0:T(4,128)(2,1)} reshape(bf16[768,3072]{1,0:T(8,128)(2,1)} %convolution_convert_fusion.1) | data formatting | bytes 9437184 | tf_op jit(solution)/shard_map/reshape | solution.py:623
  535.8 5.3 reshape.599
  554.1 160.7 %reduce_gradients.1 = (bf16[2,192,2304]{2,1,0:T(8,128)(2,1)}, bf16[2,192,768]{2,1,0:T(8,128)(2,1)}, bf16[2,192,3072]{2,1,0:T(8,128)(2,1)}, bf16[2,768,768]{2,1,0:T(8,128)(2,1)}, bf16[2,4,4,16,384]{4,3,2,1,0:T(8,128)(2,1)}) custom-call(bf16[6,4,768,768]{3,2,1,0:T(8,128)(2,1)} %fusion.3.grads, f32[4,16,384]{2,1,0:T(8,128)} %maximum_maximum_fusion.small_in), custom_call_target="tpu_custom_call" | custom-call | tf_op jit(solution)/shard_map/reduce_gradients/pallas_call | solution.py:496
  717.1 4.0 convolution_bitcast_fusion
  721.1 8.1 %copy.78 = f32[2,768,1152]{2,1,0:T(8,128)} copy(f32[2,768,1152]{1,2,0:T(8,128)} %convolution_bitcast_fusion) | data formatting | bytes 14155776
  738.0 4.4 convert_element_type.337
  (354 shorter events, 201.0 us)
Async XLA Ops:
  3.9 226.9 %copy-start.44 = (bf16[1,4,64,768]{3,2,1,0:T(8,128)(2,1)S(1)}, bf16[1,4,64,768]{3,2,1,0:T(8,128)(2,1)}, u32[]{:S(2)}) copy-start(bf16[1,4,64,768]{3,2,1,0:T(8,128)(2,1)} %param.14) | copy-start | bytes 1179652
  230.8 5.9 copy-start.63
  245.5 6.4 copy-start.21
  264.5 9.9 %copy-start.82 = (f32[256]{0:T(256)S(1)}, f32[256]{0:T(256)}, u32[]{:S(2)}) copy-start(f32[256]{0:T(256)} %get-tuple-element.77) | copy-start | bytes 3076
  274.3 6.3 copy-start.60
  274.3 6.3 slice-start
  313.2 7.2 copy-start.2
  320.4 6.4 slice-start.2
  322.5 22.2 %copy-start.12 = (f32[256,768]{1,0:T(8,128)}, f32[256,768]{1,0:T(8,128)S(1)}, u32[]{:S(2)}) copy-start(f32[256,768]{1,0:T(8,128)S(1)} %get-tuple-element.76) | copy-start | bytes 2359300
  322.5 22.2 %copy-start.72 = (f32[256]{0:T(256)}, f32[256]{0:T(256)S(1)}, u32[]{:S(2)}) copy-start(f32[256]{0:T(256)S(1)} %broadcast_multiply_fusion.2) | copy-start | bytes 3076
  322.7 22.0 %copy-start.78 = (f32[256]{0:T(256)}, f32[256]{0:T(256)S(1)}, u32[]{:S(2)}) copy-start(f32[256]{0:T(256)S(1)} %fusion.97) | copy-start | bytes 3076
  322.8 19.7 %slice-start.4 = ((s8[4718592]{0:T(1024)(128)(4,1)}), s8[4194304]{0:T(1024)(128)(4,1)S(1)}, s32[]{:S(2)}) async-start(s8[4718592]{0:T(1024)(128)(4,1)} %bitcast.246), calls=%async_computation.4 | async-start | bytes 8388608
  326.8 18.0 %copy-start.89 = (f32[256,3072]{1,0:T(8,128)}, f32[256,3072]{1,0:T(8,128)S(1)}, u32[]{:S(2)}) copy-start(f32[256,3072]{1,0:T(8,128)S(1)} %convolution_add_fusion) | copy-start | bytes 9437188
  326.8 15.6 %slice-start.5 = ((s8[4718592]{0:T(1024)(128)(4,1)}), s8[524288]{0:T(1024)(128)(4,1)S(1)}, s32[]{:S(2)}) async-start(s8[4718592]{0:T(1024)(128)(4,1)} %bitcast.246), calls=%async_computation.5 | async-start | bytes 1048576
  413.3 8.6 %copy-start.4 = (f32[256,768]{1,0:T(8,128)S(1)}, f32[256,768]{1,0:T(8,128)}, u32[]{:S(2)}) copy-start(f32[256,768]{1,0:T(8,128)} %get-tuple-element.78) | copy-start | bytes 2359300
  413.3 8.6 %copy-start.61 = (f32[256]{0:T(256)S(1)}, f32[256]{0:T(256)}, u32[]{:S(2)}) copy-start(f32[256]{0:T(256)} %copy-done.60) | copy-start | bytes 3076
  413.3 8.6 %copy-start.70 = (f32[256]{0:T(256)S(1)}, f32[256]{0:T(256)}, u32[]{:S(2)}) copy-start(f32[256]{0:T(256)} %copy-done.69) | copy-start | bytes 3076
  421.9 5.6 copy-start.18
  421.9 5.6 copy-start.24
  421.9 5.6 copy-start.38
  430.8 7.3 copy-start.22
  454.5 13.6 %copy-start.90 = (bf16[256,768]{1,0:T(8,128)(2,1)S(1)}, bf16[256,768]{1,0:T(8,128)(2,1)}, u32[]{:S(2)}) copy-start(bf16[256,768]{1,0:T(8,128)(2,1)} %get-tuple-element.94) | copy-start | bytes 1179652
  544.2 8.3 %copy-start.68 = (f32[768]{0:T(1024)S(1)}, f32[768]{0:T(1024)}, u32[]{:S(2)}) copy-start(f32[768]{0:T(1024)} %get-tuple-element.100) | copy-start | bytes 9220
  721.1 8.1 %copy-start.39 = (bf16[2,4,4,16,384]{4,3,2,1,0:T(8,128)(2,1)S(1)}, bf16[2,4,4,16,384]{4,3,2,1,0:T(8,128)(2,1)}, u32[]{:S(2)}) copy-start(bf16[2,4,4,16,384]{4,3,2,1,0:T(8,128)(2,1)} %get-tuple-element.26) | copy-start | bytes 1179652
  (73 other events, 222.4 us)
